TPU v7x, 32 devices: a whole 2x2x4 slice. The times are simulated.
32 devices in a mesh: leaf: 4 (over z), row: 8 (over y, x, core).
Axes of the slice: x: 2, y: 2, z: 4, core: 2. Of those that a mesh axis runs over, the one named last changes fastest.
Arguments:
- sub_factors: float32 [4, 2048, 512], P('leaf', 'row'), may hold values from -1 to 4, as said below
- row_values: float32 [4, 2048, 128], P('leaf', 'row'), may hold values from -1.2 to 1.2
- row_pattern: int32 [4, 32, 2], P('leaf', 'row'), may hold values 0 or 1
Outputs:
- level4_rows: float32 [2048, 512], P('row', 'leaf')
- level3_rows: float32 [256, 1792], P(('leaf', 'row'))
Inputs may be any that keep to these rules, and one draw needn't show every extreme that they name: sub_factors[i, c, r] is zero for c < r and positive for c == r.
All inputs are finite; a program needn't handle non-finite values. No bound on the sum of `row_pattern` on one device may be relied on, other than what follows from the above.
Results may differ from a plain program's by a relative error of at most 0.0003.
Values sent between devices are 32-bit elements; how exact they have to be, the bound alone decides.
A program may use at most 64 MiB of HBM per device.

v0:
```python
import jax
import jax.numpy as jnp
from jax import lax
from jax.sharding import PartitionSpec as P

PANEL = 64
SEP = 256


exact_dots = lax.Precision.HIGHEST


def broadcast(array, axis, root):
    mine = lax.axis_index(axis) == root
    return lax.psum(jnp.where(mine, array, jnp.zeros_like(array)), axis)


def swapped(array, axis, distance):
    return lax.ppermute(array, axis, [(i, i ^ 1 << distance) for i in range(lax.axis_size(axis))])


def masked_columns(values, pattern):
    col_blocks = pattern.shape[0]
    row_blocks = pattern.shape[1]
    blocks = values.reshape(col_blocks, PANEL, row_blocks, PANEL)
    flags = pattern[:, None, :, None].astype(jnp.float32)
    return (blocks * flags).reshape(values.shape)


def keep_local(operand):
    return operand


def send_four(operand, root_index):
    return broadcast(operand, "row", root_index)


def send_three(operand, root_index):
    return broadcast(operand, "row", root_index)


def eliminate(trailing, first_panel, panel_count, sender, totals, col_start):
    col_width = trailing.shape[0]
    columns = col_start + lax.iota(jnp.int32, col_width)
    pieces = []
    for panel_step in range(panel_count):
        pivot_start = (first_panel + panel_step) * PANEL
        owner_index = pivot_start // col_width
        offset = pivot_start % col_width
        panel_cols = sender(trailing[offset : offset + PANEL], owner_index)
        panel_gram = jnp.einsum(
            "im,jm->ij",
            panel_cols,
            panel_cols,
            precision=exact_dots,
            preferred_element_type=jnp.float32,
        )
        cross_terms = jnp.einsum(
            "im,cm->ic",
            panel_cols,
            trailing,
            precision=exact_dots,
            preferred_element_type=jnp.float32,
        )
        combined = totals(jnp.concatenate([panel_gram, cross_terms], axis=1))
        cholesky_low = jnp.linalg.cholesky(combined[:, :PANEL])
        coefficients = jax.scipy.linalg.solve_triangular(
            cholesky_low, combined[:, PANEL:], lower=True
        )
        coefficients = jnp.where(columns[None, :] >= pivot_start, coefficients, 0.0)
        mixing = jax.scipy.linalg.solve_triangular(cholesky_low, coefficients, lower=True, trans=1)
        trailing = trailing - jnp.einsum(
            "ic,im->cm",
            mixing,
            panel_cols,
            precision=exact_dots,
            preferred_element_type=jnp.float32,
        )
        pieces.append(coefficients.T)
    return (trailing, jnp.concatenate(pieces, axis=1))


def on_device(sub_factors, row_values, row_pattern):
    col_width = sub_factors.shape[1]
    col_start = lax.axis_index("row") * col_width
    leaf_index = lax.axis_index("leaf")
    low_pair = leaf_index % 2 == 0
    low_quad = leaf_index // 2 % 2 == 0
    factors = sub_factors[0]
    assembled = masked_columns(row_values[0], row_pattern[0])
    panel_count = SEP // PANEL
    upper_mask = jnp.where(col_start + lax.iota(jnp.int32, col_width) >= SEP, 1.0, 0.0).astype(
        jnp.float32
    )
    own_rows = jnp.concatenate([factors, assembled], axis=1)
    partner_rows = swapped(own_rows, "leaf", 0)
    first_half = jnp.where(low_pair, own_rows, partner_rows)
    second_half = jnp.where(low_pair, partner_rows, own_rows)
    stacked_rows = jnp.concatenate(
        [
            first_half[:, :SEP],
            second_half[:, :SEP],
            first_half[:, 2 * SEP :],
            second_half[:, 2 * SEP :],
        ],
        axis=1,
    )
    remainder, pivots_four = eliminate(
        stacked_rows, 0, panel_count, send_four, keep_local, col_start
    )
    contribution = (
        jnp.concatenate(
            [remainder, first_half[:, SEP : 2 * SEP], second_half[:, SEP : 2 * SEP]], axis=1
        )
        * upper_mask[:, None]
    )
    partner_child = swapped(contribution, "leaf", 1)
    merged_rows = jnp.concatenate(
        [
            jnp.where(low_quad, contribution, partner_child),
            jnp.where(low_quad, partner_child, contribution),
        ],
        axis=1,
    )
    unused, pivots_three = eliminate(
        merged_rows, panel_count, panel_count, send_three, keep_local, col_start
    )
    half_rows = SEP // 2
    four_rows = lax.dynamic_slice_in_dim(pivots_four, leaf_index % 2 * half_rows, half_rows, 1)
    quarter_rows = SEP // 4
    row_piece = lax.dynamic_slice_in_dim(
        pivots_three, leaf_index % 4 * quarter_rows, quarter_rows, 1
    )
    spread_rows = lax.all_to_all(row_piece, "row", split_axis=1, concat_axis=0, tiled=True)
    return (four_rows, spread_rows.T[:, SEP:])


def solution(mesh):
    placed = (P("leaf", "row", None), P("leaf", "row", None), P("leaf", "row", None))
    return jax.shard_map(
        on_device,
        mesh=mesh,
        in_specs=placed,
        out_specs=(P("row", "leaf"), P(("leaf", "row"), None)),
        check_vma=False,
    )
```

profile of v0, /device:TPU:0, one launch (start us, length us, event | category | flops | bytes accessed | tf_op | source)
XLA Modules:
  0.0 704.3 jit_solution(6318781128525895929)
XLA Ops:
  10.4 3.1 collective-permute-start
  13.5 14.7 %collective-permute-done = f32[256,640]{1,0:T(8,128)S(1)} collective-permute-done((f32[256,640]{1,0:T(8,128)S(1)}, f32[256,640]{1,0:T(8,128)S(1)}, u32[]{:S(2)}, u32[]{:S(2)}) %collective-permute-start) | collective-permute-done | bytes 655392 | tf_op jit(solution)/shard_map/ppermute | solution.py:19
  29.3 54.8 %all-reduce.9.cloned.1.call-done = f32[64,768]{1,0:T(8,128)} async-done(((f32[64,768]{1,0:T(8,128)}), f32[64,768]{1,0:T(8,128)}) %all-reduce.9.cloned.1.call-update) | async-done | bytes 196624 | tf_op jit(solution)/shard_map/psum | solution.py:15
  85.6 5.8 cholesky.134
  92.7 4.9 custom-call.21
  97.6 1.8 fusion.58
  99.9 1.8 convolution_subtract_fusion.6
  102.4 52.8 %all-reduce.11.cloned.1.call-done = f32[64,768]{1,0:T(8,128)} async-done(((f32[64,768]{1,0:T(8,128)}), f32[64,768]{1,0:T(8,128)}) %all-reduce.11.cloned.1.call-update) | async-done | bytes 196624 | tf_op jit(solution)/shard_map/psum | solution.py:15
  156.7 5.8 cholesky.145
  163.9 4.9 custom-call.23
  168.8 1.8 fusion.63
  174.2 52.8 %all-reduce.13.cloned.1.call-done = f32[64,768]{1,0:T(8,128)} async-done(((f32[64,768]{1,0:T(8,128)}), f32[64,768]{1,0:T(8,128)}) %all-reduce.13.cloned.1.call-update) | async-done | bytes 196624 | tf_op jit(solution)/shard_map/psum | solution.py:15
  228.5 5.8 cholesky.156
  235.7 4.9 custom-call.25
  240.6 1.8 fusion.65
  245.8 52.5 %all-reduce.15.cloned.1.call-done = f32[64,768]{1,0:T(8,128)} async-done(((f32[64,768]{1,0:T(8,128)}), f32[64,768]{1,0:T(8,128)}) %all-reduce.15.cloned.1.call-update) | async-done | bytes 196624 | tf_op jit(solution)/shard_map/psum | solution.py:15
  299.7 5.8 cholesky.167
  306.8 4.9 custom-call.27
  311.7 1.8 fusion.67
  314.0 1.8 convolution_subtract_fusion.3
  316.0 2.5 collective-permute-start.1
  318.5 56.4 %collective-permute-done.1 = f32[256,1280]{1,0:T(8,128)} collective-permute-done((f32[256,1280]{1,0:T(8,128)S(1)}, f32[256,1280]{1,0:T(8,128)}, u32[]{:S(2)}, u32[]{:S(2)}) %collective-permute-start.1) | collective-permute-done | bytes 1310752 | tf_op jit(solution)/shard_map/ppermute | solution.py:19
  374.9 1.9 broadcast_select_fusion
  377.8 54.5 %all-reduce.17.cloned.1.call-done = f32[64,2560]{1,0:T(8,128)} async-done(((f32[64,2560]{1,0:T(8,128)}), f32[64,2560]{1,0:T(8,128)}) %all-reduce.17.cloned.1.call-update) | async-done | bytes 655376 | tf_op jit(solution)/shard_map/psum | solution.py:15
  432.3 2.0 fusion.68
  434.5 5.8 cholesky.178
  441.7 4.9 custom-call.29
  446.6 3.6 fusion
  450.7 4.0 convolution_subtract_fusion.2
  455.6 54.5 %all-reduce.19.cloned.1.call-done = f32[64,2560]{1,0:T(8,128)} async-done(((f32[64,2560]{1,0:T(8,128)}), f32[64,2560]{1,0:T(8,128)}) %all-reduce.19.cloned.1.call-update) | async-done | bytes 655376 | tf_op jit(solution)/shard_map/psum | solution.py:15
  510.1 2.0 fusion.69
  512.2 5.8 cholesky.189
  519.4 5.5 custom-call.31
  524.9 3.6 fusion.70
  529.0 2.3 convolution_subtract_fusion.1
  534.0 54.3 %all-reduce.21.cloned.1.call-done = f32[64,2560]{1,0:T(8,128)} async-done(((f32[64,2560]{1,0:T(8,128)}), f32[64,2560]{1,0:T(8,128)}) %all-reduce.21.cloned.1.call-update) | async-done | bytes 655376 | tf_op jit(solution)/shard_map/psum | solution.py:15
  588.3 2.0 fusion.71
  591.1 6.6 cholesky.200
  599.0 5.5 custom-call.33
  604.5 4.5 fusion.72
  609.5 2.3 convolution_subtract_fusion
  614.3 54.5 %all-reduce.23.cloned.1.call-done = f32[64,2560]{1,0:T(8,128)} async-done(((f32[64,2560]{1,0:T(8,128)}), f32[64,2560]{1,0:T(8,128)}) %all-reduce.23.cloned.1.call-update) | async-done | bytes 655376 | tf_op jit(solution)/shard_map/psum | solution.py:15
  668.8 2.0 fusion.73
  670.8 5.8 cholesky.211
  678.0 4.9 custom-call.35
  682.9 4.5 fusion.74
  688.4 3.3 all-to-all-start
  692.6 4.1 all-to-all-done
  (146 shorter events, 41.0 us)
Async XLA Ops:
  7.2 21.1 %copy-start.9 = (f32[1,256,512]{2,1,0:T(8,128)S(1)}, f32[1,256,512]{2,1,0:T(8,128)}, u32[]{:S(2)}) copy-start(f32[1,256,512]{2,1,0:T(8,128)} %param.8) | copy-start | bytes 1572868
  7.2 77.0 %all-reduce.9.cloned.1.call-start = ((), (), s32[]{:S(2)}) async-start(), calls=%async_computation.1 | async-start | bytes 393216 | tf_op jit(solution)/shard_map/psum | solution.py:15
  10.4 17.8 %collective-permute-start = (f32[256,640]{1,0:T(8,128)S(1)}, f32[256,640]{1,0:T(8,128)S(1)}, u32[]{:S(2)}, u32[]{:S(2)}) collective-permute-start(f32[256,640]{1,0:T(8,128)S(1)} %pad_maximum_fusion.3), channel_id=1, source_target_pairs={{0,8},{8,0},{16,24},{24,16},{1,9},{9,1},{17,25},{25,17},{2,10},{10... | collective-permute-start | bytes 1966088 | tf_op jit(solution)/shard_map/ppermute | solution.py:19
  29.2 126.1 %all-reduce.11.cloned.1.call-start = ((), (), s32[]{:S(2)}) async-start(), calls=%async_computation.2 | async-start | bytes 393216 | tf_op jit(solution)/shard_map/psum | solution.py:15
  102.4 124.7 %all-reduce.13.cloned.1.call-start = ((), (), s32[]{:S(2)}) async-start(), calls=%async_computation.3 | async-start | bytes 393216 | tf_op jit(solution)/shard_map/psum | solution.py:15
  170.9 0.6 copy-start.10
  174.2 124.1 %all-reduce.15.cloned.1.call-start = ((), (), s32[]{:S(2)}) async-start(), calls=%async_computation.4 | async-start | bytes 393216 | tf_op jit(solution)/shard_map/psum | solution.py:15
  242.6 73.1 %copy-start.12 = (f32[64,256]{1,0:T(8,128)}, f32[64,256]{1,0:T(8,128)S(1)}, u32[]{:S(2)}) copy-start(f32[64,256]{1,0:T(8,128)S(1)} %convolution_select_fusion.5) | copy-start | bytes 196612
  245.3 187.0 %all-reduce.17.cloned.1.call-start = ((), (), s32[]{:S(2)}) async-start(), calls=%async_computation.5 | async-start | bytes 1310720 | tf_op jit(solution)/shard_map/psum | solution.py:15
  313.8 2.0 copy-start.14
  316.0 2.5 copy-start.8
  316.0 58.9 %collective-permute-start.1 = (f32[256,1280]{1,0:T(8,128)S(1)}, f32[256,1280]{1,0:T(8,128)}, u32[]{:S(2)}, u32[]{:S(2)}) collective-permute-start(f32[256,1280]{1,0:T(8,128)S(1)} %maximum_multiply_fusion), channel_id=1, source_target_pairs={{0,16},{8,24},{16,0},{24,8},{1,17},{9,25},{17,1},{25,9},{2,18},{10... | collective-permute-start | bytes 3932168 | tf_op jit(solution)/shard_map/ppermute | solution.py:19
  376.8 69.8 %copy-start.2 = (f32[256,1280]{1,0:T(8,128)}, f32[256,1280]{1,0:T(8,128)S(1)}, u32[]{:S(2)}) copy-start(f32[256,1280]{1,0:T(8,128)S(1)} %get-tuple-element.7) | copy-start | bytes 3932164
  376.8 69.8 %copy-start.3 = (f32[256,1280]{1,0:T(8,128)}, f32[256,1280]{1,0:T(8,128)S(1)}, u32[]{:S(2)}) copy-start(f32[256,1280]{1,0:T(8,128)S(1)} %get-tuple-element.8) | copy-start | bytes 3932164
  377.8 132.3 %all-reduce.19.cloned.1.call-start = ((), (), s32[]{:S(2)}) async-start(), calls=%async_computation.6 | async-start | bytes 1310720 | tf_op jit(solution)/shard_map/psum | solution.py:15
  432.3 18.3 %copy-start.5 = (f32[64,2560]{1,0:T(8,128)S(1)}, f32[64,2560]{1,0:T(8,128)}, u32[]{:S(2)}) copy-start(f32[64,2560]{1,0:T(8,128)} %all-reduce.17.cloned.1.call-done) | copy-start | bytes 1966084
  455.6 132.8 %all-reduce.21.cloned.1.call-start = ((), (), s32[]{:S(2)}) async-start(), calls=%async_computation.7 | async-start | bytes 1310720 | tf_op jit(solution)/shard_map/psum | solution.py:15
  510.1 18.9 %copy-start.6 = (f32[64,2560]{1,0:T(8,128)S(1)}, f32[64,2560]{1,0:T(8,128)}, u32[]{:S(2)}) copy-start(f32[64,2560]{1,0:T(8,128)} %all-reduce.19.cloned.1.call-done) | copy-start | bytes 1966084
  524.9 3.6 copy-start.16
  531.4 1.5 copy-start
  533.8 135.0 %all-reduce.23.cloned.1.call-start = ((), (), s32[]{:S(2)}) async-start(), calls=%async_computation.8 | async-start | bytes 1310720 | tf_op jit(solution)/shard_map/psum | solution.py:15
  534.0 75.5 %copy-start.1 = (f32[256,2560]{1,0:T(8,128)S(1)}, f32[256,2560]{1,0:T(8,128)}, u32[]{:S(2)}) copy-start(f32[256,2560]{1,0:T(8,128)} %copy-done) | copy-start | bytes 7864324
  588.3 21.2 %copy-start.7 = (f32[64,2560]{1,0:T(8,128)S(1)}, f32[64,2560]{1,0:T(8,128)}, u32[]{:S(2)}) copy-start(f32[64,2560]{1,0:T(8,128)} %all-reduce.21.cloned.1.call-done) | copy-start | bytes 1966084
  604.5 4.5 copy-start.17
  611.8 1.5 copy-start.4
  614.3 77.4 %copy-start.11 = (f32[64,256]{1,0:T(8,128)S(1)}, f32[64,256]{1,0:T(8,128)}, u32[]{:S(2)}) copy-start(f32[64,256]{1,0:T(8,128)} %copy-done.10) | copy-start | bytes 196612
  614.3 77.4 %copy-start.13 = (f32[64,256]{1,0:T(8,128)S(1)}, f32[64,256]{1,0:T(8,128)}, u32[]{:S(2)}) copy-start(f32[64,256]{1,0:T(8,128)} %copy-done.12) | copy-start | bytes 196612
  614.3 77.4 %copy-start.15 = (f32[64,256]{1,0:T(8,128)S(1)}, f32[64,256]{1,0:T(8,128)}, u32[]{:S(2)}) copy-start(f32[64,256]{1,0:T(8,128)} %copy-done.14) | copy-start | bytes 196612
  688.4 8.3 %all-to-all-start = ((f32[256,8,8]{0,2,1:T(8,128)}), f32[256,8,8]{0,2,1:T(8,128)S(1)}, u32[]{:S(2)}, u32[]{:S(2)}) async-start(f32[256,8,8]{0,2,1:T(8,128)} %fusion.10), calls=%async_computation | async-start | bytes 131072 | tf_op jit(solution)/shard_map/all_to_all | solution.py:134
Sparse Core Ops, SparseCore 0:
  29.3 54.7 all-reduce.8
  102.5 52.7 all-reduce.10
  174.3 52.7 all-reduce.12
  245.5 52.7 all-reduce.14
  377.9 54.4 all-reduce.16
  455.7 54.3 all-reduce.18
  533.9 54.3 all-reduce.20
  614.4 54.3 all-reduce.22
where the time goes:
time: 714 us; the launch traced here: 704 us
  waiting for transfers between devices  506 us (71%)
  other arithmetic  111 us (16%)
  matrix products  55.7 us (8%)
  between operations  15.1 us (2%)
  starting transfers between devices  9.76 us (1%)
    psum x8, waiting for transfers between devices, broadcast(): return lax.psum(jnp.where(mine, array, jnp.zeros_like(array)), axis)  431 us
    ppermute x2, waiting for transfers between devices, swapped(): lax.ppermute(array, axis, [(i, i ^ 1 << distance) for i in range(lax.axis...  71.1 us
    another operation x24, other arithmetic, eliminate(): cholesky_low = jnp.linalg.cholesky(combined[:, :PANEL])  52.9 us
    another operation x16, other arithmetic, eliminate(): jax.scipy.linalg.solve_triangular(cholesky_low, combined[:, PANEL:], lowe...  45.6 us
    dot_general x8, matrix products, eliminate(): jnp.einsum('im,cm->ic', panel_cols, trailing, precision=exact_dots, prefe...  23.3 us
    dot_general x7, matrix products, eliminate(): jnp.einsum('ic,im->cm', mixing, panel_cols, precision=exact_dots, preferr...  15.7 us
  transfers between devices with their start and end apart: 11, of which 11 were waited for; matrix products, arithmetic and copies ran while one was open for 0% of the time, Pallas kernels for 0%

commit v1 on v0

v1 whole, which is shorter than its diff:
```python
import functools

import jax
import jax.numpy as jnp
from jax import lax
from jax.experimental import pallas as pl
from jax.experimental.pallas import tpu as pltpu
from jax.sharding import PartitionSpec as P

PANEL = 64
SEP = 256
GROUP = 4
MESH = pl.DeviceIdType.MESH
exact_dots = lax.Precision.HIGHEST


def dot(left, right, left_dim, right_dim):
    return lax.dot_general(
        left,
        right,
        (((left_dim,), (right_dim,)), ((), ())),
        precision=exact_dots,
        preferred_element_type=jnp.float32,
    )


def small_factor(augmented):
    count = PANEL
    sub = lax.broadcasted_iota(jnp.int32, (8, 2 * PANEL), 0)
    live = augmented
    done = []
    for start in range(0, count, GROUP):
        offset = start % 8
        if start and offset == 0:
            done.append(live[:8])
            live = live[8:]
        cols = [
            jnp.broadcast_to(live[:, start + a : start + a + 1], live.shape) for a in range(GROUP)
        ]
        rows = [live[offset + a : offset + a + 1] for a in range(GROUP)]
        diag = [[cols[b][offset + a : offset + a + 1] for b in range(GROUP)] for a in range(GROUP)]
        factors = []
        for a in range(GROUP):
            inverse = 1.0 / diag[a][a]
            factors.append(cols[a] * inverse)
            for i in range(a + 1, GROUP):
                multiple = diag[i][a] * inverse
                rows[i] = rows[i] - multiple * rows[a]
                cols[i] = cols[i] - factors[a] * diag[a][i]
                for b in range(a + 1, GROUP):
                    diag[i][b] = diag[i][b] - multiple * diag[a][b]
        updated = live
        for a in range(GROUP):
            updated = updated - factors[a] * rows[a]
        top = jnp.where(sub >= offset + GROUP, updated[:8], live[:8])
        for a in range(GROUP):
            top = jnp.where(sub == offset + a, rows[a], top)
        live = jnp.concatenate([top, updated[8:]], axis=0) if live.shape[0] > 8 else top
    out = jnp.concatenate(done + [live], axis=0)
    row = lax.broadcasted_iota(jnp.int32, out.shape, 0)
    col = lax.broadcasted_iota(jnp.int32, out.shape, 1)
    pivots = jnp.sum(jnp.where(row == col, out, 0.0), axis=1, keepdims=True)
    return out * lax.rsqrt(pivots)


def factor_inverse(aug, gram):
    row = lax.broadcasted_iota(jnp.int32, (SEP, SEP), 0)
    col = lax.broadcasted_iota(jnp.int32, (SEP, SEP), 1)
    eye = jnp.where(row == col, 1.0, 0.0).astype(jnp.float32)
    aug[:, :SEP] = gram
    aug[:, SEP:] = eye
    for low in range(0, SEP, PANEL):
        high = low + PANEL
        square = aug[low:high, low:high]
        inverse = small_factor(jnp.concatenate([square, eye[:PANEL, :PANEL]], axis=1))[:, PANEL:]
        rows = dot(inverse, aug[low:high, :], 1, 0)
        aug[low:high, :] = rows
        if high < SEP:
            aligned = high // 128 * 128
            update = dot(rows[:, aligned:SEP], rows, 0, 0)
            aug[high:SEP, :] = aug[high:SEP, :] - update[high - aligned :]
    return aug[:, SEP:]


def kernel(
    n_row,
    own,
    four,
    three,
    piv,
    gs,
    gr,
    xs,
    xr,
    hs,
    hr,
    ys,
    yr,
    mix,
    half,
    quarter,
    halves,
    quarters,
    aug,
    raw_s,
    raw_r,
    relay_s,
    g_s,
    g_r,
    x_s,
    x_r,
    hy_s,
    hy_r,
    mix_s,
    half_s,
    quarter_s,
    down_r,
):
    leaf = lax.axis_index("leaf")
    me = lax.axis_index("row")
    width = own.shape[0]
    owners = 2 * SEP // width
    near = leaf + 1 - 2 * lax.rem(leaf, 2)
    far = leaf + 2 - 4 * lax.rem(leaf // 2, 2)
    sibling = me + 1 - 2 * lax.rem(me, 2)
    tall = own.shape[1]
    short = tall - SEP

    barrier = pltpu.get_barrier_semaphore()
    for step in range(1, n_row):
        pl.semaphore_signal(
            barrier,
            inc=1,
            device_id={"leaf": leaf, "row": lax.rem(me + step, n_row)},
            device_id_type=MESH,
        )
    for other in (near, far):
        pl.semaphore_signal(
            barrier, inc=1, device_id={"leaf": other, "row": me}, device_id_type=MESH
        )
    pl.semaphore_wait(barrier, n_row + 1)

    def remote(src, dst, send, recv, to_leaf, to_row):
        return pltpu.make_async_remote_copy(
            src_ref=src,
            dst_ref=dst,
            send_sem=send,
            recv_sem=recv,
            device_id={"leaf": to_leaf, "row": to_row},
            device_id_type=MESH,
        )

    def rows_of(block):
        return short if block * width < SEP else tall

    def raw(block, target):
        count = rows_of(block)
        return remote(
            own.at[:, pl.ds(0, count)],
            piv.at[block, :, pl.ds(0, count)],
            raw_s.at[target],
            raw_r.at[block],
            leaf,
            target,
        )

    def relay(block):
        view = piv.at[block, :, pl.ds(0, rows_of(block))]
        return remote(view, view, relay_s.at[block], raw_r.at[block], leaf, sibling)

    def raw_targets(block):
        chip, core = block // 2, block % 2
        others = [2 * q + core for q in range(n_row // 2) if q != chip]
        return [2 * chip + 1 - core] + others

    for block in range(owners):

        @pl.when(me == block)
        def _():
            for target in raw_targets(block):
                raw(block, target).start()
            piv[block] = own[...]

    for block in range(owners):

        @pl.when(me != block)
        def _():
            relay(block).wait_recv()

            @pl.when(lax.rem(me, 2) == block % 2)
            def _():
                relay(block).start()

    def pivots(first, last, count):
        blocks = [piv[b, :, :count] for b in range(first, last)]
        return blocks[0] if len(blocks) == 1 else jnp.concatenate(blocks, axis=0)

    def g_copy(i):
        return remote(gs.at[i], gr.at[i], g_s.at[i], g_r.at[i], near, me)

    def x_copy(i):
        return remote(xs.at[i], xr.at[i], x_s.at[i], x_r.at[i], near, me)

    h_copy = remote(hs, hr, hy_s.at[0], hy_r.at[0], far, me)
    y_copy = remote(ys, yr, hy_s.at[1], hy_r.at[1], far, me)
    which_half = lax.rem(leaf, 2)
    which_quarter = lax.rem(leaf, 4)

    def mix_copy(target):
        return remote(mix, mix, mix_s.at[target], down_r.at[0], leaf, target)

    def half_copy(target):
        return remote(
            halves.at[which_half], half, half_s.at[target], down_r.at[1], leaf, target
        )

    def quarter_copy(target):
        return remote(
            quarters.at[which_quarter], quarter, quarter_s.at[target], down_r.at[2], leaf, target
        )

    mid = owners // 2

    @pl.when(me == 0)
    def _():
        first = pivots(0, mid, short)
        gs[0] = dot(first, first, 1, 1)
        g_copy(0).start()
        second = pivots(mid, owners, tall)
        gs[1] = dot(first, second[:, :short], 1, 1)
        g_copy(1).start()
        gs[2] = dot(second, second, 1, 1)
        g_copy(2).start()

    xs[0] = dot(own[:, :short], pivots(0, mid, short), 1, 1)
    x_copy(0).start()
    xs[1] = dot(own[...], pivots(mid, owners, tall), 1, 1)
    x_copy(1).start()

    @pl.when(me == 0)
    def _():
        g_copy(0).wait_recv()
        inverse = factor_inverse(aug, gs[0] + gr[0])
        g_copy(1).wait_recv()
        pivot_rows = dot(inverse, gs[1] + gr[1], 1, 0)
        g_copy(2).wait_recv()
        hs[...] = gs[2] + gr[2] - dot(pivot_rows, pivot_rows, 0, 0)
        h_copy.start()
        mix[...] = dot(inverse, pivot_rows, 0, 0)
        for target in range(1, n_row):
            mix_copy(target).start()
        halves[0] = inverse[: SEP // 2]
        halves[1] = inverse[SEP // 2 :]
        for target in range(1, n_row):
            half_copy(target).start()

    @pl.when(me != 0)
    def _():
        mix_copy(0).wait_recv()

    x_copy(0).wait_recv()
    x_copy(1).wait_recv()
    cross_four = xs[0] + xr[0]
    ys[...] = xs[1] + xr[1] - dot(cross_four, mix[...], 1, 0)
    y_copy.start()

    @pl.when(me == 0)
    def _():
        h_copy.wait_recv()
        inverse = factor_inverse(aug, hs[...] + hr[...])
        for i in range(4):
            quarters[i] = inverse[i * PANEL : (i + 1) * PANEL]
        for target in range(1, n_row):
            quarter_copy(target).start()
        half[...] = halves[which_half]
        quarter[...] = quarters[which_quarter]

    @pl.when(me != 0)
    def _():
        half_copy(0).wait_recv()

    four[...] = dot(xs[0] + xr[0], half[...], 1, 1)
    y_copy.wait_recv()

    @pl.when(me != 0)
    def _():
        quarter_copy(0).wait_recv()

    three[...] = dot(ys[...] + yr[...], quarter[...], 1, 1)

    for block in range(owners):

        @pl.when(me == block)
        def _():
            for target in raw_targets(block):
                raw(block, target).wait_send()

        @pl.when(jnp.logical_and(me != block, lax.rem(me, 2) == block % 2))
        def _():
            relay(block).wait_send()

    x_copy(0).wait_send()
    x_copy(1).wait_send()
    y_copy.wait_send()

    @pl.when(me == 0)
    def _():
        for i in range(3):
            g_copy(i).wait_send()
        h_copy.wait_send()
        for target in range(1, n_row):
            mix_copy(target).wait_send()
            half_copy(target).wait_send()
            quarter_copy(target).wait_send()


def fronts(own, n_row):
    width, tall = own.shape
    owners = 2 * SEP // width
    f32 = jnp.float32
    square = pltpu.VMEM((SEP, SEP), f32)
    dma = pltpu.SemaphoreType.DMA
    vmem = pl.BlockSpec(memory_space=pltpu.VMEM)
    return pl.pallas_call(
        functools.partial(kernel, n_row),
        out_shape=(
            jax.ShapeDtypeStruct((width, SEP // 2), f32),
            jax.ShapeDtypeStruct((width, SEP // 4), f32),
        ),
        in_specs=[vmem],
        out_specs=(vmem, vmem),
        scratch_shapes=[
            pltpu.VMEM((owners, width, tall), f32),
            pltpu.VMEM((3, SEP, SEP), f32),
            pltpu.VMEM((3, SEP, SEP), f32),
            pltpu.VMEM((2, width, SEP), f32),
            pltpu.VMEM((2, width, SEP), f32),
            square,
            square,
            pltpu.VMEM((width, SEP), f32),
            pltpu.VMEM((width, SEP), f32),
            square,
            pltpu.VMEM((SEP // 2, SEP), f32),
            pltpu.VMEM((SEP // 4, SEP), f32),
            pltpu.VMEM((2, SEP // 2, SEP), f32),
            pltpu.VMEM((4, SEP // 4, SEP), f32),
            pltpu.VMEM((SEP, 2 * SEP), f32),
            dma((n_row,)),
            dma((owners,)),
            dma((owners,)),
            dma((3,)),
            dma((3,)),
            dma((2,)),
            dma((2,)),
            dma((2,)),
            dma((2,)),
            dma((n_row,)),
            dma((n_row,)),
            dma((n_row,)),
            dma((3,)),
        ],
        compiler_params=pltpu.CompilerParams(
            collective_id=0, has_side_effects=True, vmem_limit_bytes=40 * 1024 * 1024
        ),
        name="fronts",
    )(own)


def masked_columns(values, pattern):
    col_blocks = pattern.shape[0]
    row_blocks = pattern.shape[1]
    blocks = values.reshape(col_blocks, PANEL, row_blocks, PANEL)
    flags = pattern[:, None, :, None].astype(jnp.float32)
    return (blocks * flags).reshape(values.shape)


def on_device(n_row, sub_factors, row_values, row_pattern):
    factors = sub_factors[0]
    assembled = masked_columns(row_values[0], row_pattern[0])
    own = jnp.concatenate([factors[:, :SEP], assembled, factors[:, SEP:]], axis=1)
    four_rows, row_piece = fronts(own, n_row)
    spread_rows = lax.all_to_all(row_piece, "row", split_axis=1, concat_axis=0, tiled=True)
    return (four_rows, spread_rows.T[:, SEP:])


def solution(mesh):
    placed = (P("leaf", "row", None), P("leaf", "row", None), P("leaf", "row", None))
    return jax.shard_map(
        functools.partial(on_device, mesh.shape["row"]),
        mesh=mesh,
        in_specs=placed,
        out_specs=(P("row", "leaf"), P(("leaf", "row"), None)),
        check_vma=False,
    )
```

time: 714 us -> 75.6 us (0.11); the launches traced: 704 us -> 75.3 us
  waiting for transfers between devices: 506 us -> 5.02 us
  other arithmetic: 111 us -> 0.8 us
  Pallas kernels: 0 us -> 60.9 us
  matrix products: 55.7 us -> 0 us
  between operations: 15.1 us -> 0.67 us
    psum x8 -> x0, waiting for transfers between devices: 431 us -> none  [broadcast(): return lax.psum(jnp.where(mine, array, jnp.zeros_like(array)), axis)]
    another operation x40 -> x0, other arithmetic: 98.6 us -> none  [the longest x24 52.9 us: eliminate(): cholesky_low = jnp.linalg.cholesky(combined[:, :PANEL])]
    ppermute x2 -> x0, waiting for transfers between devices: 71.1 us -> none  [swapped(): lax.ppermute(array, axis, [(i, i ^ 1 << distance) for i in range(lax.axis...]
    pallas_call x0 -> x1, Pallas kernels: none -> 60.9 us  [fronts(): pl.pallas_call(functools.partial(kernel, n_row), out_shape=(jax.ShapeDtyp...]
    dot_general x23 -> x0, matrix products: 52.3 us -> none  [the longest x8 23.3 us: eliminate(): jnp.einsum('im,cm->ic', panel_cols, trailing, precision=exact_dots, prefe...]
    select_n x11 -> x0, other arithmetic: 8.39 us -> none  [the longest x8 6.41 us: broadcast(): return lax.psum(jnp.where(mine, array, jnp.zeros_like(array)), axis)]
  transfers between devices with their start and end apart: 11 -> 1, of which waited for: 11 -> 1; matrix products, arithmetic and copies ran while one was open for 0% -> 0% of each run, Pallas kernels for 0% -> 0%
where the time goes in v1:
time: 75.6 us; the launch traced here: 75.3 us
  Pallas kernels  60.9 us (81%)
  waiting for transfers between devices  5.02 us (7%)
  starting transfers between devices  4.65 us (6%)
  local copies, waits for them, and re-layouts  3.32 us (4%)
  other arithmetic  0.8 us (1%)
    pallas_call x1, Pallas kernels, fronts(): pl.pallas_call(functools.partial(kernel, n_row), out_shape=(jax.ShapeDtyp...  60.9 us
    all_to_all x1, waiting for transfers between devices, on_device(): lax.all_to_all(row_piece, 'row', split_axis=1, concat_axis=0, tiled=True)  5.02 us
    all_to_all x1, starting transfers between devices, on_device(): lax.all_to_all(row_piece, 'row', split_axis=1, concat_axis=0, tiled=True)  4.65 us
    unnamed x5, local copies, waits for them, and re-layouts  1.52 us
  transfers between devices with their start and end apart: 1, of which 1 were waited for; matrix products, arithmetic and copies ran while one was open for 0% of the time, Pallas kernels for 0%

profile of v1, /device:TPU:0, one launch (start us, length us, event | category | flops | bytes accessed | tf_op | source)
XLA Modules:
  0.0 75.3 jit_solution(16054585716404009267)
XLA Ops:
  0.6 0.0 copy-start
  0.6 0.7 convert_bitcast_fusion
  1.4 0.1 copy.7
  1.5 0.1 mul.11
  1.6 0.2 mul.12
  1.8 0.0 copy-done
  1.8 0.0 copy-start.1
  1.9 0.9 %copy-done.1 = f32[1,256,128]{2,1,0:T(8,128)S(1)} copy-done((f32[1,256,128]{2,1,0:T(8,128)S(1)}, f32[1,256,128]{2,1,0:T(8,128)}, u32[]{:S(2)}) %copy-start.1) | copy-done | bytes 131096
  2.8 60.9 %fronts.1 = (f32[256,128]{1,0:T(8,128)S(1)}, f32[256,64]{1,0:T(8,128)S(1)}) custom-call(f32[256,640]{1,0:T(8,128)S(1)} %pad_maximum_fusion.own), custom_call_target="tpu_custom_call" | custom-call | tf_op jit(solution)/shard_map/fronts/pallas_call | solution.py:324
  63.6 0.7 copy.8
  64.4 4.6 %all-to-all-start = ((f32[256,8,8]{0,2,1:T(8,128)}), f32[256,8,8]{0,2,1:T(8,128)S(1)}, u32[]{:S(2)}, u32[]{:S(2)}) async-start(f32[256,8,8]{0,2,1:T(8,128)} %bitcast.3), calls=%async_computation | async-start | bytes 131072 | tf_op jit(solution)/shard_map/all_to_all | solution.py:382
  69.0 5.0 %all-to-all-done = f32[256,8,8]{0,2,1:T(8,128)S(1)} async-done(((f32[256,8,8]{0,2,1:T(8,128)}), f32[256,8,8]{0,2,1:T(8,128)S(1)}, u32[]{:S(2)}, u32[]{:S(2)}) %all-to-all-start) | async-done | bytes 65568 | tf_op jit(solution)/shard_map/all_to_all | solution.py:382
  74.0 0.6 slice.14
  74.7 0.7 copy.10
  (3 shorter events, 0.1 us)
Async XLA Ops:
  0.6 1.2 %copy-start = (f32[1,256,512]{2,1,0:T(8,128)S(1)}, f32[1,256,512]{2,1,0:T(8,128)}, u32[]{:S(2)}) copy-start(f32[1,256,512]{2,1,0:T(8,128)} %param.3) | copy-start | bytes 1572868
  1.8 0.9 %copy-start.1 = (f32[1,256,128]{2,1,0:T(8,128)S(1)}, f32[1,256,128]{2,1,0:T(8,128)}, u32[]{:S(2)}) copy-start(f32[1,256,128]{2,1,0:T(8,128)} %param.4) | copy-start | bytes 393220
  64.4 9.7 %all-to-all-start = ((f32[256,8,8]{0,2,1:T(8,128)}), f32[256,8,8]{0,2,1:T(8,128)S(1)}, u32[]{:S(2)}, u32[]{:S(2)}) async-start(f32[256,8,8]{0,2,1:T(8,128)} %bitcast.3), calls=%async_computation | async-start | bytes 131072 | tf_op jit(solution)/shard_map/all_to_all | solution.py:382

commit v2 on v1

--- a/solution.py
+++ b/solution.py
@@ -9,7 +9,7 @@
 
 PANEL = 64
 SEP = 256
-GROUP = 4
+GROUP = 8
 MESH = pl.DeviceIdType.MESH
 exact_dots = lax.Precision.HIGHEST
 
@@ -102,9 +102,12 @@
     halves,
     quarters,
     aug,
+    ts,
+    tr,
     raw_s,
     raw_r,
     relay_s,
+    onward_s,
     g_s,
     g_r,
     x_s,
@@ -115,6 +118,8 @@
     half_s,
     quarter_s,
     down_r,
+    spread_s,
+    spread_r,
 ):
     leaf = lax.axis_index("leaf")
     me = lax.axis_index("row")
@@ -153,50 +158,92 @@
     def rows_of(block):
         return short if block * width < SEP else tall
 
-    def raw(block, target):
-        count = rows_of(block)
+    def part_view(ref, block, part):
+        return ref.at[pl.ds(part * (width // 2), width // 2), pl.ds(0, rows_of(block))]
+
+    def raw(block, part, target):
         return remote(
-            own.at[:, pl.ds(0, count)],
-            piv.at[block, :, pl.ds(0, count)],
-            raw_s.at[target],
-            raw_r.at[block],
+            part_view(own, block, part),
+            part_view(piv.at[block], block, part),
+            raw_s.at[2 * target + part],
+            raw_r.at[2 * block + part],
             leaf,
             target,
         )
 
-    def relay(block):
-        view = piv.at[block, :, pl.ds(0, rows_of(block))]
-        return remote(view, view, relay_s.at[block], raw_r.at[block], leaf, sibling)
-
-    def raw_targets(block):
+    def pass_on(block, part, send, target):
+        view = part_view(piv.at[block], block, part)
+        return remote(view, view, send, raw_r.at[2 * block + part], leaf, target)
+
+    def relay(block, part):
+        return pass_on(block, part, relay_s.at[2 * block + part], sibling)
+
+    def onward(block, part):
+        return pass_on(block, part, onward_s.at[block], 6 + block % 2)
+
+    square_plane = n_row == 8
+
+    def raw_sends(block):
         chip, core = block // 2, block % 2
+        sends = [(2 * chip + 1 - core, 0), (2 * chip + 1 - core, 1)]
+        if square_plane:
+            return sends + [(2 + core, 0), (4 + core, 1), (2 + core, 1), (4 + core, 0)]
         others = [2 * q + core for q in range(n_row // 2) if q != chip]
-        return [2 * chip + 1 - core] + others
+        return sends + [(target, part) for target in others for part in range(2)]
+
+    def arrive(block, part):
+        relay(block, part).wait_recv()
+
+        @pl.when(lax.rem(me, 2) == block % 2)
+        def _():
+            relay(block, part).start()
+
+        if square_plane:
+
+            @pl.when(me == 2 + 2 * part + block % 2)
+            def _():
+                onward(block, part).start()
+
+    def g_copy(i):
+        return remote(gs.at[i], gr.at[i], g_s.at[i], g_r.at[i], near, me)
+
+    mid = owners // 2
 
     for block in range(owners):
 
         @pl.when(me == block)
         def _():
-            for target in raw_targets(block):
-                raw(block, target).start()
+            for target, part in raw_sends(block):
+                raw(block, part, target).start()
             piv[block] = own[...]
+            if block == 0 and mid == 1:
+                gs[0] = dot(own[:, :short], own[:, :short], 1, 1)
+                g_copy(0).start()
 
     for block in range(owners):
 
         @pl.when(me != block)
         def _():
-            relay(block).wait_recv()
-
-            @pl.when(lax.rem(me, 2) == block % 2)
-            def _():
-                relay(block).start()
+            if square_plane:
+                late = me == 4 + block % 2
+
+                @pl.when(late)
+                def _():
+                    arrive(block, 1)
+                    arrive(block, 0)
+
+                @pl.when(jnp.logical_not(late))
+                def _():
+                    arrive(block, 0)
+                    arrive(block, 1)
+
+            else:
+                arrive(block, 0)
+                arrive(block, 1)
 
     def pivots(first, last, count):
         blocks = [piv[b, :, :count] for b in range(first, last)]
         return blocks[0] if len(blocks) == 1 else jnp.concatenate(blocks, axis=0)
-
-    def g_copy(i):
-        return remote(gs.at[i], gr.at[i], g_s.at[i], g_r.at[i], near, me)
 
     def x_copy(i):
         return remote(xs.at[i], xr.at[i], x_s.at[i], x_r.at[i], near, me)
@@ -219,13 +266,12 @@
             quarters.at[which_quarter], quarter, quarter_s.at[target], down_r.at[2], leaf, target
         )
 
-    mid = owners // 2
-
     @pl.when(me == 0)
     def _():
         first = pivots(0, mid, short)
-        gs[0] = dot(first, first, 1, 1)
-        g_copy(0).start()
+        if mid > 1:
+            gs[0] = dot(first, first, 1, 1)
+            g_copy(0).start()
         second = pivots(mid, owners, tall)
         gs[1] = dot(first, second[:, :short], 1, 1)
         g_copy(1).start()
@@ -286,18 +332,58 @@
     def _():
         quarter_copy(0).wait_recv()
 
-    three[...] = dot(ys[...] + yr[...], quarter[...], 1, 1)
+    spread = dot(quarter[...], ys[...] + yr[...], 1, 1)
+    share = PANEL // n_row
+    for target in range(n_row):
+        ts[target] = spread[target * share : (target + 1) * share]
+
+    def spread_copy(source, target):
+        return remote(
+            ts.at[target], tr.at[source], spread_s.at[target], spread_r.at[source], leaf, target
+        )
+
+    for target in range(n_row):
+
+        @pl.when(jnp.logical_and(me >= mid, me != target))
+        def _():
+            spread_copy(me, target).start()
+
+    for source in range(mid, n_row):
+
+        @pl.when(me == source)
+        def _():
+            tr[source] = ts[source]
+
+        @pl.when(me != source)
+        def _():
+            spread_copy(source, source).wait_recv()
+
+    three[...] = jnp.concatenate([tr[source] for source in range(mid, n_row)], axis=1)
+
+    for target in range(n_row):
+
+        @pl.when(jnp.logical_and(me >= mid, me != target))
+        def _():
+            spread_copy(me, target).wait_send()
 
     for block in range(owners):
 
         @pl.when(me == block)
         def _():
-            for target in raw_targets(block):
-                raw(block, target).wait_send()
+            for target, part in raw_sends(block):
+                raw(block, part, target).wait_send()
 
         @pl.when(jnp.logical_and(me != block, lax.rem(me, 2) == block % 2))
         def _():
-            relay(block).wait_send()
+            for part in range(2):
+                relay(block, part).wait_send()
+
+        if square_plane:
+            for part in range(2):
+
+                @pl.when(me == 2 + 2 * part + block % 2)
+                def _():
+                    onward(block, part).wait_send()
 
     x_copy(0).wait_send()
     x_copy(1).wait_send()
@@ -325,7 +411,7 @@
         functools.partial(kernel, n_row),
         out_shape=(
             jax.ShapeDtypeStruct((width, SEP // 2), f32),
-            jax.ShapeDtypeStruct((width, SEP // 4), f32),
+            jax.ShapeDtypeStruct((SEP // 4 // n_row, width * n_row - SEP), f32),
         ),
         in_specs=[vmem],
         out_specs=(vmem, vmem),
@@ -345,8 +431,11 @@
             pltpu.VMEM((2, SEP // 2, SEP), f32),
             pltpu.VMEM((4, SEP // 4, SEP), f32),
             pltpu.VMEM((SEP, 2 * SEP), f32),
-            dma((n_row,)),
-            dma((owners,)),
+            pltpu.VMEM((n_row, SEP // 4 // n_row, width), f32),
+            pltpu.VMEM((n_row, SEP // 4 // n_row, width), f32),
+            dma((2 * n_row,)),
+            dma((2 * owners,)),
+            dma((2 * owners,)),
             dma((owners,)),
             dma((3,)),
             dma((3,)),
@@ -358,6 +447,8 @@
             dma((n_row,)),
             dma((n_row,)),
             dma((3,)),
+            dma((n_row,)),
+            dma((n_row,)),
         ],
         compiler_params=pltpu.CompilerParams(
             collective_id=0, has_side_effects=True, vmem_limit_bytes=40 * 1024 * 1024
@@ -378,9 +469,7 @@
     factors = sub_factors[0]
     assembled = masked_columns(row_values[0], row_pattern[0])
     own = jnp.concatenate([factors[:, :SEP], assembled, factors[:, SEP:]], axis=1)
-    four_rows, row_piece = fronts(own, n_row)
-    spread_rows = lax.all_to_all(row_piece, "row", split_axis=1, concat_axis=0, tiled=True)
-    return (four_rows, spread_rows.T[:, SEP:])
+    return fronts(own, n_row)
 
 
 def solution(mesh):

time: 75.6 us -> 63.5 us (0.84)
  waiting for transfers between devices: 5.02 us -> 0 us
  starting transfers between devices: 4.65 us -> 0 us
  Pallas kernels: 60.9 us -> 59.5 us
    all_to_all x1 -> x0, waiting for transfers between devices: 5.02 us -> none  [on_device(): lax.all_to_all(row_piece, 'row', split_axis=1, concat_axis=0, tiled=True)]
    all_to_all x1 -> x0, starting transfers between devices: 4.65 us -> none  [on_device(): lax.all_to_all(row_piece, 'row', split_axis=1, concat_axis=0, tiled=True)]
    pallas_call x1, Pallas kernels: 60.9 us -> 59.5 us  [fronts(): pl.pallas_call(functools.partial(kernel, n_row), out_shape=(jax.ShapeDtyp...]
    unnamed x5 -> x8, local copies, waits for them, and re-layouts: 1.52 us -> 2.7 us
  transfers between devices with their start and end apart: 1 -> 0, of which waited for: 1 -> 0; matrix products, arithmetic and copies ran while one was open for 0% -> 0% of each run, Pallas kernels for 0% -> 0%
where the time goes in v2:
time: 63.5 us; the launch traced here: 63.4 us
  Pallas kernels  59.5 us (94%)
  local copies, waits for them, and re-layouts  3.15 us (5%)
  between operations  0.69 us (1%)
    pallas_call x1, Pallas kernels, fronts(): pl.pallas_call(functools.partial(kernel, n_row), out_shape=(jax.ShapeDtyp...  59.5 us
    unnamed x8, local copies, waits for them, and re-layouts  2.7 us

profile of v2, /device:TPU:0, one launch (start us, length us, event | category | flops | bytes accessed | tf_op | source)
XLA Modules:
  0.0 63.4 jit_solution(10746336019652819615)
XLA Ops:
  0.6 0.0 copy-start.2
  0.6 0.7 %copy-done.2 = s32[1,4,2]{1,2,0:T(2,128)S(1)} copy-done((s32[1,4,2]{1,2,0:T(2,128)S(1)}, s32[1,4,2]{1,2,0:T(2,128)}, u32[]{:S(2)}) %copy-start.2) | copy-done | bytes 56
  1.3 0.1 copy.5
  1.4 0.0 copy-start
  1.4 0.1 mul.11
  1.6 0.0 copy-start.1
  1.6 0.2 mul.12
  1.8 0.7 %copy-done.1 = f32[1,256,128]{2,1,0:T(8,128)S(1)} copy-done((f32[1,256,128]{2,1,0:T(8,128)S(1)}, f32[1,256,128]{2,1,0:T(8,128)}, u32[]{:S(2)}) %copy-start.1) | copy-done | bytes 131096
  2.5 0.0 copy-done
  2.6 59.5 %fronts.1 = (f32[256,128]{1,0:T(8,128)S(1)}, f32[8,1792]{1,0:T(8,128)S(1)}) custom-call(f32[256,640]{1,0:T(8,128)S(1)} %pad_maximum_fusion.own), custom_call_target="tpu_custom_call" | custom-call | tf_op jit(solution)/shard_map/fronts/pallas_call | solution.py:410
  62.1 0.7 %copy.8 = f32[256,128]{1,0:T(8,128)} copy(f32[256,128]{1,0:T(8,128)S(1)} %get-tuple-element.6) | data formatting | bytes 262144
  62.7 0.6 copy.9
  (4 shorter events, 0.1 us)
Async XLA Ops:
  0.6 0.7 %copy-start.2 = (s32[1,4,2]{1,2,0:T(2,128)S(1)}, s32[1,4,2]{1,2,0:T(2,128)}, u32[]{:S(2)}) copy-start(s32[1,4,2]{1,2,0:T(2,128)} %param.5) | copy-start | bytes 100
  1.4 1.1 %copy-start = (f32[1,256,512]{2,1,0:T(8,128)S(1)}, f32[1,256,512]{2,1,0:T(8,128)}, u32[]{:S(2)}) copy-start(f32[1,256,512]{2,1,0:T(8,128)} %param.3) | copy-start | bytes 1572868
  1.6 0.9 %copy-start.1 = (f32[1,256,128]{2,1,0:T(8,128)S(1)}, f32[1,256,128]{2,1,0:T(8,128)}, u32[]{:S(2)}) copy-start(f32[1,256,128]{2,1,0:T(8,128)} %param.4) | copy-start | bytes 393220

commit v3 on v2

--- a/solution.py
+++ b/solution.py
@@ -261,6 +261,15 @@
             halves.at[which_half], half, half_s.at[target], down_r.at[1], leaf, target
         )
 
+    def mix_relay():
+        return remote(mix, mix, mix_s.at[0], down_r.at[0], leaf, sibling)
+
+    def half_relay():
+        return remote(half, half, half_s.at[0], down_r.at[1], leaf, sibling)
+
+    relaying = jnp.logical_and(me != 0, lax.rem(me, 2) == 0)
+    first_targets = [1] + list(range(2, n_row, 2))
+
     def quarter_copy(target):
         return remote(
             quarters.at[which_quarter], quarter, quarter_s.at[target], down_r.at[2], leaf, target
@@ -280,8 +289,11 @@
 
     xs[0] = dot(own[:, :short], pivots(0, mid, short), 1, 1)
     x_copy(0).start()
-    xs[1] = dot(own[...], pivots(mid, owners, tall), 1, 1)
-    x_copy(1).start()
+
+    @pl.when(me >= mid)
+    def _():
+        xs[1] = dot(own[...], pivots(mid, owners, tall), 1, 1)
+        x_copy(1).start()
 
     @pl.when(me == 0)
     def _():
@@ -293,26 +305,33 @@
         hs[...] = gs[2] + gr[2] - dot(pivot_rows, pivot_rows, 0, 0)
         h_copy.start()
         mix[...] = dot(inverse, pivot_rows, 0, 0)
-        for target in range(1, n_row):
+        for target in first_targets:
             mix_copy(target).start()
         halves[0] = inverse[: SEP // 2]
         halves[1] = inverse[SEP // 2 :]
-        for target in range(1, n_row):
+
+    @pl.when(me != 0)
+    def _():
+        mix_copy(0).wait_recv()
+
+    @pl.when(relaying)
+    def _():
+        mix_relay().start()
+
+    x_copy(0).wait_recv()
+
+    @pl.when(me >= mid)
+    def _():
+        correction = dot(xs[0] + xr[0], mix[...], 1, 0)
+        x_copy(1).wait_recv()
+        ys[...] = xs[1] + xr[1] - correction
+        y_copy.start()
+
+    @pl.when(me == 0)
+    def _():
+        h_copy.wait_recv()
+        for target in first_targets:
             half_copy(target).start()
-
-    @pl.when(me != 0)
-    def _():
-        mix_copy(0).wait_recv()
-
-    x_copy(0).wait_recv()
-    x_copy(1).wait_recv()
-    cross_four = xs[0] + xr[0]
-    ys[...] = xs[1] + xr[1] - dot(cross_four, mix[...], 1, 0)
-    y_copy.start()
-
-    @pl.when(me == 0)
-    def _():
-        h_copy.wait_recv()
         inverse = factor_inverse(aug, hs[...] + hr[...])
         for i in range(4):
             quarters[i] = inverse[i * PANEL : (i + 1) * PANEL]
@@ -325,17 +344,24 @@
     def _():
         half_copy(0).wait_recv()
 
+    @pl.when(relaying)
+    def _():
+        half_relay().start()
+
     four[...] = dot(xs[0] + xr[0], half[...], 1, 1)
-    y_copy.wait_recv()
 
     @pl.when(me != 0)
     def _():
         quarter_copy(0).wait_recv()
 
-    spread = dot(quarter[...], ys[...] + yr[...], 1, 1)
     share = PANEL // n_row
-    for target in range(n_row):
-        ts[target] = spread[target * share : (target + 1) * share]
+
+    @pl.when(me >= mid)
+    def _():
+        y_copy.wait_recv()
+        spread = dot(quarter[...], ys[...] + yr[...], 1, 1)
+        for target in range(n_row):
+            ts[target] = spread[target * share : (target + 1) * share]
 
     def spread_copy(source, target):
         return remote(
@@ -386,18 +412,27 @@
                     onward(block, part).wait_send()
 
     x_copy(0).wait_send()
-    x_copy(1).wait_send()
-    y_copy.wait_send()
+
+    @pl.when(me >= mid)
+    def _():
+        x_copy(1).wait_send()
+        y_copy.wait_send()
 
     @pl.when(me == 0)
     def _():
         for i in range(3):
             g_copy(i).wait_send()
         h_copy.wait_send()
-        for target in range(1, n_row):
+        for target in first_targets:
             mix_copy(target).wait_send()
             half_copy(target).wait_send()
+        for target in range(1, n_row):
             quarter_copy(target).wait_send()
+
+    @pl.when(relaying)
+    def _():
+        mix_relay().wait_send()
+        half_relay().wait_send()
 
 
 def fronts(own, n_row):

time: 63.5 us -> 62 us (0.976)
  Pallas kernels: 59.5 us -> 57.9 us
    pallas_call x1, Pallas kernels: 59.5 us -> 57.9 us  [fronts(): pl.pallas_call(functools.partial(kernel, n_row), out_shape=(jax.ShapeDtyp...]
where the time goes in v3:
time: 62 us; the launch traced here: 61.8 us
  Pallas kernels  57.9 us (93%)
  local copies, waits for them, and re-layouts  3.15 us (5%)
  between operations  0.69 us (1%)
    pallas_call x1, Pallas kernels, fronts(): pl.pallas_call(functools.partial(kernel, n_row), out_shape=(jax.ShapeDtyp...  57.9 us
    unnamed x8, local copies, waits for them, and re-layouts  2.7 us

profile of v3, /device:TPU:0, one launch (start us, length us, event | category | flops | bytes accessed | tf_op | source)
XLA Modules:
  0.0 61.8 jit_solution(17103738112388079380)
XLA Ops:
  0.6 0.0 copy-start.2
  0.6 0.7 %copy-done.2 = s32[1,4,2]{1,2,0:T(2,128)S(1)} copy-done((s32[1,4,2]{1,2,0:T(2,128)S(1)}, s32[1,4,2]{1,2,0:T(2,128)}, u32[]{:S(2)}) %copy-start.2) | copy-done | bytes 56
  1.3 0.1 copy.5
  1.4 0.0 copy-start
  1.4 0.1 mul.11
  1.6 0.0 copy-start.1
  1.6 0.2 mul.12
  1.8 0.7 %copy-done.1 = f32[1,256,128]{2,1,0:T(8,128)S(1)} copy-done((f32[1,256,128]{2,1,0:T(8,128)S(1)}, f32[1,256,128]{2,1,0:T(8,128)}, u32[]{:S(2)}) %copy-start.1) | copy-done | bytes 131096
  2.5 0.0 copy-done
  2.6 57.9 %fronts.1 = (f32[256,128]{1,0:T(8,128)S(1)}, f32[8,1792]{1,0:T(8,128)S(1)}) custom-call(f32[256,640]{1,0:T(8,128)S(1)} %pad_maximum_fusion.own), custom_call_target="tpu_custom_call" | custom-call | tf_op jit(solution)/shard_map/fronts/pallas_call | solution.py:445
  60.5 0.7 %copy.8 = f32[256,128]{1,0:T(8,128)} copy(f32[256,128]{1,0:T(8,128)S(1)} %get-tuple-element.6) | data formatting | bytes 262144
  61.2 0.6 %copy.9 = f32[8,1792]{1,0:T(8,128)} copy(f32[8,1792]{1,0:T(8,128)S(1)} %get-tuple-element.7) | data formatting | bytes 114688
  (4 shorter events, 0.1 us)
Async XLA Ops:
  0.6 0.7 %copy-start.2 = (s32[1,4,2]{1,2,0:T(2,128)S(1)}, s32[1,4,2]{1,2,0:T(2,128)}, u32[]{:S(2)}) copy-start(s32[1,4,2]{1,2,0:T(2,128)} %param.5) | copy-start | bytes 100
  1.4 1.1 %copy-start = (f32[1,256,512]{2,1,0:T(8,128)S(1)}, f32[1,256,512]{2,1,0:T(8,128)}, u32[]{:S(2)}) copy-start(f32[1,256,512]{2,1,0:T(8,128)} %param.3) | copy-start | bytes 1572868
  1.6 0.9 %copy-start.1 = (f32[1,256,128]{2,1,0:T(8,128)S(1)}, f32[1,256,128]{2,1,0:T(8,128)}, u32[]{:S(2)}) copy-start(f32[1,256,128]{2,1,0:T(8,128)} %param.4) | copy-start | bytes 393220
